TPU v7x, 32 devices: a whole 2x2x4 slice. The times are simulated.
32 devices in a mesh: dp: 16 (over z, y, core), ctx: 2 (over x).
Axes of the slice: x: 2, y: 2, z: 4, core: 2. Of those that a mesh axis runs over, the one named last changes fastest.
Arguments:
- query_heads: bfloat16 [16, 256, 4096], P('dp', 'ctx'), may hold values from -160 to 160
- key_heads: bfloat16 [16, 256, 512], P('dp', 'ctx'), may hold values from -6 to 6
- value_heads: bfloat16 [16, 256, 512], P('dp', 'ctx'), may hold values from -6 to 6
- out_grad: bfloat16 [16, 256, 4096], P('dp', 'ctx'), may hold values from -6 to 6
- layer_inputs: bfloat16 [16, 256, 8192], P('dp', 'ctx'), may hold values from -6 to 6
- doc_lengths: int32 [16, 8], P('dp'), may hold values from 1 to 128, 256 in all within a row
Outputs:
- query_grad: bfloat16 [16, 256, 4096], P('dp', 'ctx')
- key_grad: bfloat16 [16, 256, 512], P('dp', 'ctx')
- value_grad: bfloat16 [16, 256, 512], P('dp', 'ctx')
- weight_grad: float32 [8192, 512], P(('dp', 'ctx'))
All inputs are finite; a program needn't handle non-finite values.
Results may differ from a plain program's by a relative error of at most 0.0053.
Values may be sent and summed in bfloat16 or wider, within the bound.
A program may use at most 128 MiB of HBM per device.

v0:
```python
import jax
import jax.numpy as jnp
from jax import lax
from jax.sharding import PartitionSpec as P

HD = 128
HEADS = 32
KVH = 4


NEG_FILL = -1e30


def document_ids(lengths_row, length):
    endings = jnp.cumsum(lengths_row)
    positions = jnp.arange(length, dtype=jnp.int32)
    return jnp.sum((positions[:, None] >= endings[None, :]).astype(jnp.int32), axis=1)


def shards(query_heads, key_heads, value_heads, out_grad, layer_inputs, doc_lengths):
    queries_here = query_heads[0]
    rows_here = queries_here.shape[0]
    shard_count = lax.axis_size("ctx")
    data_count = lax.axis_size("dp")
    length = rows_here * shard_count
    group_size = HEADS // KVH
    softmax_scale = HD ** (-0.5)
    key_width = key_heads.shape[2]
    key_all, value_all = (
        lax.all_gather(key_heads[0], "ctx", axis=0, tiled=True),
        lax.all_gather(value_heads[0], "ctx", axis=0, tiled=True),
    )
    documents = document_ids(doc_lengths[0], length)
    first_row = lax.axis_index("ctx") * rows_here
    positions = jnp.arange(length, dtype=jnp.int32)
    query_pos = first_row + jnp.arange(rows_here, dtype=jnp.int32)
    query_docs = lax.dynamic_slice_in_dim(documents, first_row, rows_here)
    allowed = (query_docs[:, None] == documents[None, :]) & (
        positions[None, :] <= query_pos[:, None]
    )
    query_split = queries_here.reshape(rows_here, KVH, group_size, HD)
    key_split = key_all.reshape(length, KVH, HD)
    value_split = value_all.reshape(length, KVH, HD)
    grad_split = out_grad[0].reshape(rows_here, KVH, group_size, HD)
    scores = (
        jnp.einsum("igsd,jgd->gsij", query_split, key_split, preferred_element_type=jnp.float32)
        * softmax_scale
    )
    scores = jnp.where(allowed[None, None], scores, NEG_FILL)
    row_top = jnp.max(scores, axis=-1, keepdims=True)
    row_total = jnp.sum(jnp.exp(scores - row_top), axis=-1, keepdims=True)
    probability = jnp.exp(scores - (row_top + jnp.log(row_total)))
    prob_low = probability.astype(jnp.bfloat16)
    attended = jnp.einsum(
        "gsij,jgd->igsd", prob_low, value_split, preferred_element_type=jnp.float32
    )
    delta = jnp.transpose(jnp.sum(grad_split.astype(jnp.float32) * attended, axis=-1), (1, 2, 0))
    dprob = jnp.einsum(
        "igsd,jgd->gsij", grad_split, value_split, preferred_element_type=jnp.float32
    )
    dscore_low = (probability * (dprob - delta[..., None])).astype(jnp.bfloat16)
    query_grad = (
        jnp.einsum("gsij,jgd->igsd", dscore_low, key_split, preferred_element_type=jnp.float32)
        * softmax_scale
    )
    query_grad = query_grad.reshape(rows_here, HEADS * HD).astype(jnp.bfloat16)
    key_term = (
        jnp.einsum("gsij,igsd->jgd", dscore_low, query_split, preferred_element_type=jnp.float32)
        * softmax_scale
    )
    value_term = jnp.einsum(
        "gsij,igsd->jgd", prob_low, grad_split, preferred_element_type=jnp.float32
    )
    summed_grads = lax.psum_scatter(
        jnp.concatenate(
            [
                key_term.reshape(lax.axis_size("ctx") * rows_here, key_width),
                value_term.reshape(lax.axis_size("ctx") * rows_here, key_width),
            ],
            axis=1,
        ),
        "ctx",
        scatter_dimension=0,
        tiled=True,
    )
    key_grad = summed_grads[:, :key_width].astype(jnp.bfloat16)
    value_grad = summed_grads[:, key_width:].astype(jnp.bfloat16)
    inputs_here = layer_inputs[0]
    weight_grad = lax.psum_scatter(
        jnp.einsum("te,tc->ec", inputs_here, value_grad, preferred_element_type=jnp.float32),
        ("dp", "ctx"),
        scatter_dimension=0,
        tiled=True,
    )
    weight_grad = weight_grad * (data_count * length) ** (-0.5)
    return (query_grad[None], key_grad[None], value_grad[None], weight_grad)


def solution(mesh):
    placed = (
        P("dp", "ctx", None),
        P("dp", "ctx", None),
        P("dp", "ctx", None),
        P("dp", "ctx", None),
        P("dp", "ctx", None),
        P("dp", None),
    )
    return jax.shard_map(
        shards,
        mesh=mesh,
        in_specs=placed,
        out_specs=(
            P("dp", "ctx", None),
            P("dp", "ctx", None),
            P("dp", "ctx", None),
            P(("dp", "ctx"), None),
        ),
        check_vma=False,
    )
```

profile of v0, /device:TPU:11, one launch (start us, length us, event | category | flops | bytes accessed | tf_op | source)
XLA Modules:
  0.0 438.1 jit_solution(11325262847346848987)
XLA Ops:
  7.2 0.0 copy-start
  7.2 0.0 reduce-scatter.3.cloned.1.call-start
  7.2 1.0 reduce-window.8
  8.2 0.1 convert_reduce_fusion
  8.3 1.0 copy.40
  9.3 5.1 %all-gather = bf16[1,256,512]{1,2,0:T(8,128)(2,1)S(1)} all-gather(bf16[1,128,512]{1,2,0:T(8,128)(2,1)S(1)} %copy.40), channel_id=2, replica_groups=mesh['dp'=16,'ctx'=2] {'ctx'}, dimensions={1}, use_global_device_ids=true | all-gather | bytes 393216 | tf_op jit(solution)/shard_map/all_gather | solution.py:30
  14.4 1.0 copy.43
  15.4 4.6 %all-gather.1 = bf16[1,256,512]{1,2,0:T(8,128)(2,1)} all-gather(bf16[1,128,512]{1,2,0:T(8,128)(2,1)S(1)} %copy.43), channel_id=3, replica_groups=mesh['dp'=16,'ctx'=2] {'ctx'}, dimensions={1}, use_global_device_ids=true | all-gather | bytes 393216 | tf_op jit(solution)/shard_map/all_gather | solution.py:31
  20.1 1.6 copy.71
  21.7 2.3 copy.44
  24.0 0.1 dynamic_slice.3
  24.0 0.1 fusion.7
  24.1 0.0 copy-start.3
  24.2 0.8 fusion.3
  24.9 0.9 exponential_reduce_fusion
  25.9 0.0 copy-start.4
  25.9 0.0 copy-done.3
  25.9 1.8 fusion.9
  27.7 0.0 copy-done.4
  27.8 1.2 fusion.5
  29.0 1.5 fusion.1
  30.5 0.0 copy-start.1
  30.5 1.6 fusion.6
  32.1 0.0 copy-done.1
  32.1 1.2 copy.52
  33.3 1.2 copy.53
  34.6 1.1 pad_maximum_fusion
  35.6 0.0 reduce-scatter.3.cloned.1.call-update
  35.7 0.0 reduce-scatter.5.cloned.1.call-start
  35.7 22.6 %reduce-scatter.3.cloned.1.call-done = f32[128,1024]{1,0:T(8,128)} async-done(((f32[256,1024]{1,0:T(8,128)}), f32[128,1024]{1,0:T(8,128)}) %reduce-scatter.3.cloned.1.call-update) | async-done | bytes 524304 | tf_op jit(solution)/shard_map/reduce_scatter | solution.py:74
  58.3 1.1 convert.4
  59.4 0.0 copy-start.2
  59.4 0.7 copy-done.2
  60.1 0.0 copy-done
  60.1 8.1 %convolution_bitcast_fusion = f32[8192,512]{0,1:T(8,128)} fusion(bf16[1,128,8192]{2,1,0:T(8,128)(2,1)S(1)} %copy-done, bf16[128,1024]{1,0:T(8,128)(2,1)S(1)} %convert.4), kind=kOutput, calls=%fused_computation | convolution fusion | flops 1073741824 | bytes 19005440 | tf_op jit(solution)/shard_map/te,tc->ec/dot_general | solution.py:90
  68.2 0.0 reduce-scatter.5.cloned.1.call-update
  68.2 2.1 multiply_convert_fusion
  70.3 1.3 copy.54
  71.6 1.7 slice_bitcast_fusion.1
  73.3 355.9 %reduce-scatter.5.cloned.1.call-done = f32[256,512]{0,1:T(8,128)} async-done(((f32[8192,512]{0,1:T(8,128)}), f32[256,512]{0,1:T(8,128)}) %reduce-scatter.5.cloned.1.call-update) | async-done | bytes 524304 | tf_op jit(solution)/shard_map/reduce_scatter | solution.py:89
  429.2 1.1 broadcast_multiply_fusion
  430.2 1.0 copy.55
  (2 shorter events, 0.0 us)
Async XLA Ops:
  7.2 53.0 %copy-start = (bf16[1,128,8192]{2,1,0:T(8,128)(2,1)S(1)}, bf16[1,128,8192]{2,1,0:T(8,128)(2,1)}, u32[]{:S(2)}) copy-start(bf16[1,128,8192]{2,1,0:T(8,128)(2,1)} %param.10) | copy-start | bytes 6291460
  7.2 51.2 %reduce-scatter.3.cloned.1.call-start = ((), (), s32[]{:S(2)}) async-start(), calls=%async_computation.2 | async-start | bytes 1572864 | tf_op jit(solution)/shard_map/reduce_scatter | solution.py:74
  24.1 1.8 copy-start.3
  25.9 1.9 copy-start.4
  30.5 1.6 copy-start.1
  35.7 393.5 %reduce-scatter.5.cloned.1.call-start = ((), (), s32[]{:S(2)}) async-start(), calls=%async_computation.3 | async-start | bytes 17301504 | tf_op jit(solution)/shard_map/reduce_scatter | solution.py:89
  59.4 0.7 copy-start.2
Sparse Core Ops, SparseCore 0:
  35.8 22.5 reduce-scatter.2
  68.4 360.7 reduce-scatter.4
where the time goes:
time: 439 us; the launch traced here: 438 us
  waiting for transfers between devices  379 us (86%)
  matrix products  17.1 us (4%)
  between operations  14.2 us (3%)
  local copies, waits for them, and re-layouts  13.2 us (3%)
  blocking collectives  9.72 us (2%)
  other arithmetic  5.31 us (1%)
    reduce_scatter x1, waiting for transfers between devices, shards(): lax.psum_scatter(jnp.einsum('te,tc->ec', inputs_here, value_grad, preferr...  356 us
    reduce_scatter x1, waiting for transfers between devices, shards(): lax.psum_scatter(jnp.concatenate([key_term.reshape(lax.axis_size('ctx') *...  22.6 us
  transfers between devices with their start and end apart: 2, of which 2 were waited for; matrix products, arithmetic and copies ran while one was open for 1% of the time, Pallas kernels for 0%

commit v1 on v0

--- a/solution.py
+++ b/solution.py
@@ -1,14 +1,342 @@
+import functools
+
 import jax
 import jax.numpy as jnp
 from jax import lax
+from jax.experimental import pallas as pl
+from jax.experimental.pallas import tpu as pltpu
 from jax.sharding import PartitionSpec as P
 
 HD = 128
 HEADS = 32
 KVH = 4
+GROUP = HEADS // KVH
+PAIR = 2
+PLANE = 8
+F32 = jnp.float32
+BF16 = jnp.bfloat16
+MESH = pl.DeviceIdType.MESH
 
 
 NEG_FILL = -1e30
+
+
+def nt(a, b):
+    return lax.dot_general(a, b, (((1,), (1,)), ((), ())), preferred_element_type=F32)
+
+
+def nn(a, b):
+    return jnp.dot(a, b, preferred_element_type=F32)
+
+
+def cols(index, width=HD):
+    return pl.ds(pl.multiple_of(index * width, width), width)
+
+
+def target_orders(depth):
+    table = []
+    for z in range(depth):
+        up = list(range(depth - 1, z, -1))
+        down = list(range(z))
+        first, second = (up, down) if z < depth // 2 else (down, up)
+        order = []
+        while first or second:
+            if first:
+                order.append(first.pop(0))
+            if second:
+                order.append(second.pop(0))
+        table.append(order + [z])
+    return table
+
+
+def documents_of(lengths, shape, axis, first):
+    positions = lax.broadcasted_iota(jnp.int32, shape, axis) + first
+    found = jnp.zeros(shape, jnp.int32)
+    ending = jnp.int32(0)
+    for number in range(lengths.shape[1]):
+        ending = ending + lengths[0, number]
+        found = found + (positions >= ending).astype(jnp.int32)
+    return positions, found
+
+
+def kernel(
+    depth, out_scale,
+    q_ref, k_ref, v_ref, go_ref, x_ref, len_ref,
+    dq_ref, dk_ref, dv_ref, w_ref,
+    k_prev, v_prev, bias, term_k, term_v, sum_k, sum_v,
+    x_all, dvt_all, w_send, w_recv, w_own,
+    kv_send, kv_recv, term_send, term_recv,
+    x_send, x_recv, x_local, dv_send, dv_recv, ws_send, ws_recv,
+):
+    rows = q_ref.shape[0]
+    dp = lax.axis_index("dp")
+    ctx = lax.axis_index("ctx")
+    lanes = PLANE // 2
+    z = dp // lanes
+    me = (dp % lanes) * 2 + ctx
+    width = w_ref.shape[0]
+    scale = HD ** -0.5
+
+    def peer(offset):
+        other = (me + offset) % PLANE
+        return other, (z * lanes + other // 2, other % 2)
+
+    above = (dp + lanes, ctx)
+    below = (dp - lanes, ctx)
+    partner = (dp, 1 - ctx)
+    last = depth - 1
+
+    barrier = pltpu.get_barrier_semaphore()
+    for offset in range(1, PLANE):
+        pl.semaphore_signal(barrier, inc=1, device_id=peer(offset)[1], device_id_type=MESH)
+
+    @pl.when(z > 0)
+    def _():
+        pl.semaphore_signal(barrier, inc=1, device_id=below, device_id_type=MESH)
+
+    @pl.when(z < last)
+    def _():
+        pl.semaphore_signal(barrier, inc=1, device_id=above, device_id_type=MESH)
+
+    line = (z > 0).astype(jnp.int32) + (z < last).astype(jnp.int32)
+    pl.semaphore_wait(barrier, PLANE - 1 + line)
+
+    def remote(src, dst, send, recv, device):
+        return pltpu.make_async_remote_copy(
+            src_ref=src, dst_ref=dst, send_sem=send, recv_sem=recv,
+            device_id=device, device_id_type=MESH,
+        )
+
+    def kv_copies():
+        return (
+            remote(k_ref, k_prev, kv_send.at[0], kv_recv.at[0], partner),
+            remote(v_ref, v_prev, kv_send.at[1], kv_recv.at[1], partner),
+        )
+
+    def term_copy(part):
+        buffer = (term_v, term_k)[part]
+        return remote(buffer, buffer, term_send.at[part], term_recv.at[part], partner)
+
+    @pl.when(ctx == 0)
+    def _():
+        for copy in kv_copies():
+            copy.start()
+
+    table = target_orders(depth)
+    targets = []
+    for step in range(depth):
+        target = jnp.int32(0)
+        for place in range(depth):
+            target = target + (z == place).astype(jnp.int32) * table[place][step]
+        targets.append(target)
+
+    def x_copy(target, offset, sender, receiver, device):
+        return remote(
+            x_ref.at[:, cols(target * PLANE + receiver, width)],
+            x_all.at[target, pl.ds(pl.multiple_of(sender * rows, rows), rows)],
+            x_send.at[target, offset - 1], x_recv.at[target, offset - 1], device,
+        )
+
+    def own_copy(target):
+        return pltpu.make_async_copy(
+            x_ref.at[:, cols(target * PLANE + me, width)],
+            x_all.at[target, pl.ds(pl.multiple_of(me * rows, rows), rows)],
+            x_local.at[target],
+        )
+
+    for target in targets:
+        for offset in range(1, PLANE):
+            other, device = peer(offset)
+            x_copy(target, offset, me, other, device).start()
+        own_copy(target).start()
+
+    def attend(blocks):
+        length = blocks * rows
+        shape = (length, rows)
+        first = ctx * rows
+        query_pos, query_docs = documents_of(len_ref, shape, 1, first)
+        key_pos, key_docs = documents_of(len_ref, shape, 0, first - (blocks - 1) * rows)
+        allowed = (query_docs == key_docs) & (key_pos <= query_pos)
+        bias[:length] = jnp.where(allowed, 0.0, NEG_FILL)
+
+        def group(g, carry):
+            here = cols(g)
+            key_part, value_part = k_ref[:, here], v_ref[:, here]
+            if blocks == 2:
+                key_part = jnp.concatenate([k_prev[:, here], key_part], axis=0)
+                value_part = jnp.concatenate([v_prev[:, here], value_part], axis=0)
+            key_turned = key_part.astype(F32).T.astype(BF16)
+            key_sum = jnp.zeros((length, HD), F32)
+            value_sum = jnp.zeros((length, HD), F32)
+            mask = jnp.concatenate([bias[:length]] * PAIR, axis=1)
+            for pair in range(GROUP // PAIR):
+                heads = [cols(g * GROUP + pair * PAIR + i) for i in range(PAIR)]
+                query = jnp.concatenate([q_ref[:, h] for h in heads], axis=0)
+                grad = jnp.concatenate([go_ref[:, h] for h in heads], axis=0)
+                scores = nt(key_part, query) * scale + mask
+                top = jnp.max(scores, axis=0, keepdims=True)
+                weight = jnp.exp(scores - top)
+                prob = weight * (1.0 / jnp.sum(weight, axis=0, keepdims=True))
+                prob_low = prob.astype(BF16)
+                dprob = nt(value_part, grad)
+                delta = jnp.sum(prob_low.astype(F32) * dprob, axis=0, keepdims=True)
+                dscore = (prob * (dprob - delta)).astype(BF16)
+                value_sum = value_sum + nn(prob_low, grad)
+                key_sum = key_sum + nn(dscore, query)
+                turned = nn(key_turned, dscore) * scale
+                for i, h in enumerate(heads):
+                    dq_ref[:, h] = turned[:, i * rows:(i + 1) * rows].T.astype(BF16)
+            key_sum = key_sum * scale
+            if blocks == 2:
+                term_k[:, here] = key_sum[:rows].astype(BF16)
+                term_v[:, here] = value_sum[:rows].astype(BF16)
+                dk_ref[:, here] = key_sum[rows:].astype(BF16)
+                dv_ref[:, here] = value_sum[rows:].astype(BF16)
+                dvt_all[here, cols(me, rows)] = value_sum[rows:].T.astype(BF16)
+            else:
+                sum_k[:, here] = key_sum
+                sum_v[:, here] = value_sum
+            return carry
+
+        lax.fori_loop(0, KVH, group, 0)
+
+    @pl.when(ctx == 0)
+    def _():
+        attend(1)
+        term_copy(0).wait_recv()
+        for g in range(KVH):
+            here = pl.ds(g * HD, HD)
+            total = sum_v[:, here] + term_v[:, here].astype(F32)
+            dv_ref[:, here] = total.astype(BF16)
+            dvt_all[here, cols(me, rows)] = total.T.astype(BF16)
+
+    @pl.when(ctx == 1)
+    def _():
+        for copy in kv_copies():
+            copy.wait_recv()
+        attend(2)
+        for part in range(2):
+            term_copy(part).start()
+
+    def dv_copy(offset, sender, device):
+        return remote(
+            dvt_all.at[:, cols(sender, rows)], dvt_all.at[:, cols(sender, rows)],
+            dv_send.at[offset - 1], dv_recv.at[offset - 1], device,
+        )
+
+    for offset in range(1, PLANE):
+        dv_copy(offset, me, peer(offset)[1]).start()
+
+    @pl.when(ctx == 0)
+    def _():
+        term_copy(1).wait_recv()
+        dk_ref[...] = (sum_k[...] + term_k[...].astype(F32)).astype(BF16)
+
+    for offset in range(1, PLANE):
+        sender = (me + PLANE - offset) % PLANE
+        dv_copy(offset, sender, peer(offset)[1]).wait_recv()
+
+    def w_up(target):
+        return remote(w_send.at[target], w_recv.at[0, target], ws_send.at[target], ws_recv.at[0, target], above)
+
+    def w_down(target):
+        return remote(w_send.at[target], w_recv.at[1, target], ws_send.at[target], ws_recv.at[1, target], below)
+
+    for target in targets:
+        for offset in range(1, PLANE):
+            sender = (me + PLANE - offset) % PLANE
+            other, device = peer(offset)
+            x_copy(target, offset, sender, me, device).wait_recv()
+        own_copy(target).wait()
+        w_own[...] = nn(dvt_all[...], x_all[target])
+
+        @pl.when((z > 0) & (target >= z))
+        def _():
+            w_up(target).wait_recv()
+            w_own[...] += w_recv[0, target].astype(F32)
+
+        @pl.when((z < last) & (target <= z))
+        def _():
+            w_down(target).wait_recv()
+            w_own[...] += w_recv[1, target].astype(F32)
+
+        @pl.when(target > z)
+        def _():
+            w_send[target] = w_own[...].astype(BF16)
+            w_up(target).start()
+
+        @pl.when(target < z)
+        def _():
+            w_send[target] = w_own[...].astype(BF16)
+            w_down(target).start()
+
+    w_ref[...] = (w_own[...] * out_scale).T
+
+    for target in targets:
+        for offset in range(1, PLANE):
+            other, device = peer(offset)
+            x_copy(target, offset, me, other, device).wait_send()
+
+        @pl.when(target != z)
+        def _():
+            w_up(target).wait_send()
+
+    for offset in range(1, PLANE):
+        dv_copy(offset, me, peer(offset)[1]).wait_send()
+
+    @pl.when(ctx == 0)
+    def _():
+        for copy in kv_copies():
+            copy.wait_send()
+
+    @pl.when(ctx == 1)
+    def _():
+        for part in range(2):
+            term_copy(part).wait_send()
+
+
+def fused(query_heads, key_heads, value_heads, out_grad, layer_inputs, doc_lengths):
+    rows, model = layer_inputs.shape[1:]
+    key_width = key_heads.shape[2]
+    count = lax.axis_size("dp") * lax.axis_size("ctx")
+    depth = count // PLANE
+    width = model // count
+    out_scale = (lax.axis_size("dp") * lax.axis_size("ctx") * rows) ** (-0.5)
+    vmem = pl.BlockSpec(memory_space=pltpu.VMEM)
+    dma = pltpu.SemaphoreType.DMA
+    query_grad, key_grad, value_grad, weight_grad = pl.pallas_call(
+        functools.partial(kernel, depth, out_scale),
+        out_shape=(
+            jax.ShapeDtypeStruct(query_heads.shape[1:], BF16),
+            jax.ShapeDtypeStruct((rows, key_width), BF16),
+            jax.ShapeDtypeStruct((rows, key_width), BF16),
+            jax.ShapeDtypeStruct((width, key_width), F32),
+        ),
+        in_specs=[vmem] * 4 + [pl.BlockSpec(memory_space=pl.ANY), pl.BlockSpec(memory_space=pltpu.SMEM)],
+        out_specs=(vmem,) * 4,
+        scratch_shapes=[
+            pltpu.VMEM((rows, key_width), BF16),
+            pltpu.VMEM((rows, key_width), BF16),
+            pltpu.VMEM((2 * rows, rows), F32),
+            pltpu.VMEM((rows, key_width), BF16),
+            pltpu.VMEM((rows, key_width), BF16),
+            pltpu.VMEM((rows, key_width), F32),
+            pltpu.VMEM((rows, key_width), F32),
+            pltpu.VMEM((depth, PLANE * rows, width), BF16),
+            pltpu.VMEM((key_width, PLANE * rows), BF16),
+            pltpu.VMEM((depth, key_width, width), BF16),
+            pltpu.VMEM((2, depth, key_width, width), BF16),
+            pltpu.VMEM((key_width, width), F32),
+            dma((2,)), dma((2,)), dma((2,)), dma((2,)),
+            dma((depth, PLANE - 1)), dma((depth, PLANE - 1)), dma((depth,)),
+            dma((PLANE - 1,)), dma((PLANE - 1,)),
+            dma((depth,)), dma((2, depth)),
+        ],
+        compiler_params=pltpu.CompilerParams(
+            collective_id=0, has_side_effects=True, vmem_limit_bytes=48 * 1024 * 1024
+        ),
+    )(query_heads[0], key_heads[0], value_heads[0], out_grad[0], layer_inputs[0], doc_lengths)
+    return (query_grad[None], key_grad[None], value_grad[None], weight_grad)
 
 
 def document_ids(lengths_row, length):
@@ -96,6 +424,16 @@
     return (query_grad[None], key_grad[None], value_grad[None], weight_grad)
 
 
+def place(query_heads, key_heads, value_heads, out_grad, layer_inputs, doc_lengths):
+    arrays = (query_heads, key_heads, value_heads, out_grad, layer_inputs, doc_lengths)
+    rows, model = layer_inputs.shape[1:]
+    count = lax.axis_size("dp") * lax.axis_size("ctx")
+    whole_tiles = rows % HD == 0 and model % (count * HD) == 0
+    if lax.axis_size("ctx") == 2 and count % PLANE == 0 and whole_tiles:
+        return fused(*arrays)
+    return shards(*arrays)
+
+
 def solution(mesh):
     placed = (
         P("dp", "ctx", None),
@@ -106,7 +444,7 @@
         P("dp", None),
     )
     return jax.shard_map(
-        shards,
+        place,
         mesh=mesh,
         in_specs=placed,
         out_specs=(

time: 439 us -> 78 us (0.18)
  the two profiles are of different devices: /device:TPU:11 before, /device:TPU:7 now
where the time goes in v1:
time: 78 us; the launch traced here: 77.7 us
  Pallas kernels  69.1 us (89%)
  local copies, waits for them, and re-layouts  7.98 us (10%)
    pallas_call x1, Pallas kernels, fused(): pl.pallas_call(functools.partial(kernel, depth, out_scale), out_shape=(ja...  69.1 us
    unnamed x14, local copies, waits for them, and re-layouts  7.98 us

profile of v1, /device:TPU:7, one launch (start us, length us, event | category | flops | bytes accessed | tf_op | source)
XLA Modules:
  0.0 77.7 jit_solution(18140749998422990244)
XLA Ops:
  0.6 0.0 copy-start
  0.6 1.2 %copy-done = bf16[1,128,4096]{2,1,0:T(8,128)(2,1)S(1)} copy-done((bf16[1,128,4096]{2,1,0:T(8,128)(2,1)S(1)}, bf16[1,128,4096]{2,1,0:T(8,128)(2,1)}, u32[]{:S(2)}) %copy-start) | copy-done | bytes 1048600
  1.9 0.0 copy-start.1
  1.9 1.2 %copy-done.1 = bf16[1,128,4096]{2,1,0:T(8,128)(2,1)S(1)} copy-done((bf16[1,128,4096]{2,1,0:T(8,128)(2,1)S(1)}, bf16[1,128,4096]{2,1,0:T(8,128)(2,1)}, u32[]{:S(2)}) %copy-start.1) | copy-done | bytes 1048600
  3.1 0.0 copy-start.2
  3.1 0.9 %copy-done.2 = bf16[1,128,512]{2,1,0:T(8,128)(2,1)S(1)} copy-done((bf16[1,128,512]{2,1,0:T(8,128)(2,1)S(1)}, bf16[1,128,512]{2,1,0:T(8,128)(2,1)}, u32[]{:S(2)}) %copy-start.2) | copy-done | bytes 131096
  4.0 0.0 copy-start.3
  4.0 0.9 %copy-done.3 = bf16[1,128,512]{2,1,0:T(8,128)(2,1)S(1)} copy-done((bf16[1,128,512]{2,1,0:T(8,128)(2,1)S(1)}, bf16[1,128,512]{2,1,0:T(8,128)(2,1)}, u32[]{:S(2)}) %copy-start.3) | copy-done | bytes 131096
  4.9 0.0 copy-start.4
  4.9 0.7 copy-done.4
  5.5 69.1 %shard_map.93 = (bf16[128,4096]{1,0:T(8,128)(2,1)S(1)}, bf16[128,512]{1,0:T(8,128)(2,1)S(1)}, bf16[128,512]{1,0:T(8,128)(2,1)S(1)}, f32[256,512]{1,0:T(8,128)S(1)}) custom-call(bf16[128,4096]{1,0:T(8,128)(2,1)S(1)} %bitcast.8, bf16[128,512]{1,0:T(8,128)(2,1)S(1)} %bitcast.11, bf16[128,512]{1,0:T(8,128)(2,1)S(1)} %bitcast.12, bf16[128,4096]{1,0:T(8,128)(2,1)S(1)} %bitcast.9, ...), custom_call_target="tpu_custom_call" | custom-call | tf_op jit(solution)/shard_map/pallas_call | solution.py:307
  74.7 1.0 %copy.14 = bf16[1,128,4096]{2,1,0:T(8,128)(2,1)} copy(bf16[1,128,4096]{2,1,0:T(8,128)(2,1)S(1)} %bitcast.10) | data formatting | bytes 2097152
  75.6 0.7 copy.15
  76.3 0.7 copy.16
  77.0 0.8 %copy.17 = f32[256,512]{1,0:T(8,128)} copy(f32[256,512]{1,0:T(8,128)S(1)} %get-tuple-element.19) | data formatting | bytes 1048576
Async XLA Ops:
  0.6 1.2 %copy-start = (bf16[1,128,4096]{2,1,0:T(8,128)(2,1)S(1)}, bf16[1,128,4096]{2,1,0:T(8,128)(2,1)}, u32[]{:S(2)}) copy-start(bf16[1,128,4096]{2,1,0:T(8,128)(2,1)} %param.6) | copy-start | bytes 3145732
  1.9 1.2 %copy-start.1 = (bf16[1,128,4096]{2,1,0:T(8,128)(2,1)S(1)}, bf16[1,128,4096]{2,1,0:T(8,128)(2,1)}, u32[]{:S(2)}) copy-start(bf16[1,128,4096]{2,1,0:T(8,128)(2,1)} %param.9) | copy-start | bytes 3145732
  3.1 0.9 %copy-start.2 = (bf16[1,128,512]{2,1,0:T(8,128)(2,1)S(1)}, bf16[1,128,512]{2,1,0:T(8,128)(2,1)}, u32[]{:S(2)}) copy-start(bf16[1,128,512]{2,1,0:T(8,128)(2,1)} %param.7) | copy-start | bytes 393220
  4.0 0.9 %copy-start.3 = (bf16[1,128,512]{2,1,0:T(8,128)(2,1)S(1)}, bf16[1,128,512]{2,1,0:T(8,128)(2,1)}, u32[]{:S(2)}) copy-start(bf16[1,128,512]{2,1,0:T(8,128)(2,1)} %param.8) | copy-start | bytes 393220
  4.9 0.7 copy-start.4

commit v2 on v0

--- a/solution.py
+++ b/solution.py
@@ -1,14 +1,353 @@
+import functools
+import math
+
 import jax
 import jax.numpy as jnp
 from jax import lax
+from jax.experimental import pallas as pl
+from jax.experimental.pallas import tpu as pltpu
 from jax.sharding import PartitionSpec as P
 
 HD = 128
 HEADS = 32
 KVH = 4
+GROUP = HEADS // KVH
+PAIR = 2
+PLANE = 8
+LOG2E = math.log2(math.e)
+F32 = jnp.float32
+BF16 = jnp.bfloat16
+MESH = pl.DeviceIdType.MESH
 
 
 NEG_FILL = -1e30
+
+
+def nt(a, b):
+    return lax.dot_general(a, b, (((1,), (1,)), ((), ())), preferred_element_type=F32)
+
+
+def nn(a, b):
+    return jnp.dot(a, b, preferred_element_type=F32)
+
+
+def cols(index, width=HD):
+    return pl.ds(pl.multiple_of(index * width, width), width)
+
+
+def target_orders(depth):
+    table = []
+    for z in range(depth):
+        others = [t for t in range(depth) if t != z]
+        others.sort(key=lambda t: (-abs(t - z), t))
+        table.append(others + [z])
+    return table
+
+
+def documents_of(lengths, shape, axis, first):
+    positions = lax.broadcasted_iota(jnp.int32, shape, axis) + first
+    found = jnp.zeros(shape, jnp.int32)
+    ending = jnp.int32(0)
+    for number in range(lengths.shape[1]):
+        ending = ending + lengths[0, number]
+        found = found + (positions >= ending).astype(jnp.int32)
+    return positions, found
+
+
+def kernel(
+    depth, out_scale,
+    q_hbm, k_hbm, v_hbm, go_hbm, x_ref, len_ref,
+    dq_ref, dk_ref, dv_ref, w_ref,
+    q_ref, k_ref, v_ref, go_ref, k_prev, v_prev, bias, term_k, term_v,
+    x_all, dvt_all, w_send, w_recv, w_own,
+    in_sem, kv_send, kv_recv, term_send, term_recv,
+    x_send, x_recv, x_local, dv_send, dv_recv, ws_send, ws_recv,
+):
+    rows = q_ref.shape[0]
+    dp = lax.axis_index("dp")
+    ctx = lax.axis_index("ctx")
+    lanes = PLANE // 2
+    z = dp // lanes
+    lane = dp % lanes
+    me = lane * 2 + ctx
+    width = w_ref.shape[0]
+    scale = HD ** -0.5
+
+    inputs = [
+        pltpu.make_async_copy(src, dst, in_sem.at[i])
+        for i, (src, dst) in enumerate(
+            [(k_hbm, k_ref), (v_hbm, v_ref), (q_hbm, q_ref), (go_hbm, go_ref)]
+        )
+    ]
+    for copy in inputs:
+        copy.start()
+
+    def peer(offset):
+        other = (me + offset) % PLANE
+        return other, (z * lanes + other // 2, other % 2)
+
+    def level(target):
+        return (target * lanes + lane, ctx)
+
+    partner = (dp, 1 - ctx)
+
+    barrier = pltpu.get_barrier_semaphore()
+    for offset in range(1, PLANE):
+        pl.semaphore_signal(barrier, inc=1, device_id=peer(offset)[1], device_id_type=MESH)
+    for step in range(1, depth):
+        pl.semaphore_signal(barrier, inc=1, device_id=level((z + step) % depth), device_id_type=MESH)
+    pl.semaphore_wait(barrier, PLANE - 1 + depth - 1)
+
+    def remote(src, dst, send, recv, device):
+        return pltpu.make_async_remote_copy(
+            src_ref=src, dst_ref=dst, send_sem=send, recv_sem=recv,
+            device_id=device, device_id_type=MESH,
+        )
+
+    def kv_copy(g, part):
+        src, dst = ((k_hbm, k_prev), (v_hbm, v_prev))[part]
+        here = cols(g)
+        return remote(src.at[:, here], dst.at[:, here], kv_send.at[part, g], kv_recv.at[part, g], partner)
+
+    def term_copy(g, part):
+        buffer = (term_v, term_k)[part].at[g]
+        return remote(buffer, buffer, term_send.at[part, g], term_recv.at[part, g], partner)
+
+    def x_copy(target, offset, sender, receiver, device):
+        return remote(
+            x_ref.at[:, cols(target * PLANE + receiver, width)],
+            x_all.at[target, pl.ds(pl.multiple_of(sender * rows, rows), rows)],
+            x_send.at[target, offset - 1], x_recv.at[target, offset - 1], device,
+        )
+
+    def own_copy(target):
+        return pltpu.make_async_copy(
+            x_ref.at[:, cols(target * PLANE + me, width)],
+            x_all.at[target, pl.ds(pl.multiple_of(me * rows, rows), rows)],
+            x_local.at[target],
+        )
+
+    def dv_copy(g, offset, sender, device):
+        place = dvt_all.at[cols(g), cols(sender, rows)]
+        return remote(place, place, dv_send.at[g, offset - 1], dv_recv.at[g, offset - 1], device)
+
+    def w_copy(g, source, target):
+        here = cols(g)
+        return remote(
+            w_send.at[target, here], w_recv.at[source, here],
+            ws_send.at[target, g], ws_recv.at[source, g], level(target),
+        )
+
+    table = target_orders(depth)
+
+    def target_at(step):
+        target = jnp.int32(0)
+        for place in range(depth):
+            for number in range(depth):
+                here = ((z == place) & (step == number)).astype(jnp.int32)
+                target = target + here * table[place][number]
+        return target
+
+    @pl.when(ctx == 0)
+    def _():
+        for g in range(KVH):
+            for part in range(2):
+                kv_copy(g, part).start()
+
+    targets = [target_at(step) for step in range(depth)]
+    for target in targets:
+        for offset in range(2, PLANE, 2):
+            other, device = peer(offset)
+            x_copy(target, offset, me, other, device).start()
+        own_copy(target).start()
+
+    @pl.when(ctx == 0)
+    def _():
+        for g in range(KVH):
+            for part in range(2):
+                kv_copy(g, part).wait_send()
+
+    for target in targets:
+        for offset in range(1, PLANE, 2):
+            other, device = peer(offset)
+            x_copy(target, offset, me, other, device).start()
+
+    for copy in inputs:
+        copy.wait()
+
+    shape = (2 * rows, rows)
+    first = ctx * rows
+    query_pos, query_docs = documents_of(len_ref, shape, 1, first)
+    key_pos, key_docs = documents_of(len_ref, shape, 0, first - rows)
+    allowed = (query_docs == key_docs) & (key_pos <= query_pos)
+    bias[...] = jnp.where(allowed, 0.0, NEG_FILL)
+
+    def attend(g, blocks):
+        length = blocks * rows
+        here = cols(g)
+        key_part, value_part = k_ref[:, here], v_ref[:, here]
+        if blocks == 2:
+            key_part = jnp.concatenate([k_prev[:, here], key_part], axis=0)
+            value_part = jnp.concatenate([v_prev[:, here], value_part], axis=0)
+        key_turned = key_part.astype(F32).T.astype(BF16)
+        key_sum = jnp.zeros((length, HD), F32)
+        value_sum = jnp.zeros((length, HD), F32)
+        mask = jnp.concatenate([bias[2 * rows - length:]] * PAIR, axis=1)
+        for pair in range(GROUP // PAIR):
+            heads = [cols(g * GROUP + pair * PAIR + i) for i in range(PAIR)]
+            query = jnp.concatenate([q_ref[:, h] for h in heads], axis=0)
+            grad = jnp.concatenate([go_ref[:, h] for h in heads], axis=0)
+            scores = nt(key_part, query) * (scale * LOG2E) + mask
+            top = jnp.max(scores, axis=0, keepdims=True)
+            weight = jnp.exp2(scores - top)
+            prob = weight * (1.0 / jnp.sum(weight, axis=0, keepdims=True))
+            prob_low = prob.astype(BF16)
+            dprob = nt(value_part, grad)
+            delta = jnp.sum(prob_low.astype(F32) * dprob, axis=0, keepdims=True)
+            dscore = (prob * (dprob - delta)).astype(BF16)
+            value_sum = value_sum + nn(prob_low, grad)
+            key_sum = key_sum + nn(dscore, query)
+            turned = nn(key_turned, dscore) * scale
+            for i, h in enumerate(heads):
+                dq_ref[:, h] = turned[:, i * rows:(i + 1) * rows].T.astype(BF16)
+        return key_sum * scale, value_sum
+
+    def finish(g, key_sum, value_sum):
+        here = cols(g)
+        dk_ref[:, here] = key_sum.astype(BF16)
+        dv_ref[:, here] = value_sum.astype(BF16)
+        dvt_all[here, cols(me, rows)] = value_sum.T.astype(BF16)
+
+    def shell(m):
+        for offset in range(1, PLANE):
+            sender = (me + PLANE - offset) % PLANE
+            dv_copy(m, offset, sender, peer(offset)[1]).wait_recv()
+
+        def block(i, carry):
+            old = (i < m).astype(jnp.int32)
+            step = old * i + (1 - old) * m
+            g = old * m + (1 - old) * (i - m)
+            target = target_at(step)
+
+            @pl.when(i == m)
+            def _():
+                x_wait(target)
+
+            product = nn(dvt_all[cols(g)], x_all[target])
+            w_send[target, cols(g)] = product.astype(BF16)
+            w_copy(g, z, target).start()
+            return carry
+
+        last = (m == depth - 1).astype(jnp.int32)
+        lax.fori_loop(0, 2 * m + 1 - last * (m + 1), block, 0)
+
+    def x_wait(target):
+        for offset in range(1, PLANE):
+            sender = (me + PLANE - offset) % PLANE
+            x_copy(target, offset, sender, me, peer(offset)[1]).wait_recv()
+        own_copy(target).wait()
+
+    def group(g, carry):
+        @pl.when(ctx == 0)
+        def _():
+            key_sum, value_sum = attend(g, 1)
+            for part in range(2):
+                term_copy(g, part).wait_recv()
+            finish(g, key_sum + term_k[g].astype(F32), value_sum + term_v[g].astype(F32))
+
+        @pl.when(ctx == 1)
+        def _():
+            for part in range(2):
+                kv_copy(g, part).wait_recv()
+            key_sum, value_sum = attend(g, 2)
+            term_v[g] = value_sum[:rows].astype(BF16)
+            term_k[g] = key_sum[:rows].astype(BF16)
+            for part in range(2):
+                term_copy(g, part).start()
+            finish(g, key_sum[rows:], value_sum[rows:])
+
+        for offset in range(1, PLANE):
+            dv_copy(g, offset, me, peer(offset)[1]).start()
+
+        @pl.when(g > 0)
+        def _():
+            shell(g - 1)
+
+        return carry
+
+    lax.fori_loop(0, KVH, group, 0)
+    shell(jnp.int32(KVH - 1))
+    x_wait(z)
+    w_own[...] = nn(dvt_all[...], x_all[z])
+    for step in range(1, depth):
+        source = (z + step) % depth
+        for g in range(KVH):
+            w_copy(g, source, z).wait_recv()
+        w_own[...] += w_recv[source].astype(F32)
+    w_ref[...] = (w_own[...] * out_scale).T
+
+    for target in targets:
+        for offset in range(1, PLANE):
+            other, device = peer(offset)
+            x_copy(target, offset, me, other, device).wait_send()
+    for step in range(1, depth):
+        for g in range(KVH):
+            w_copy(g, z, (z + step) % depth).wait_send()
+    for g in range(KVH):
+        for offset in range(1, PLANE):
+            dv_copy(g, offset, me, peer(offset)[1]).wait_send()
+
+    @pl.when(ctx == 1)
+    def _():
+        for g in range(KVH):
+            for part in range(2):
+                term_copy(g, part).wait_send()
+
+
+def fused(query_heads, key_heads, value_heads, out_grad, layer_inputs, doc_lengths):
+    rows, model = layer_inputs.shape[1:]
+    key_width = key_heads.shape[2]
+    count = lax.axis_size("dp") * lax.axis_size("ctx")
+    depth = count // PLANE
+    width = model // count
+    out_scale = (lax.axis_size("dp") * lax.axis_size("ctx") * rows) ** (-0.5)
+    vmem = pl.BlockSpec(memory_space=pltpu.VMEM)
+    dma = pltpu.SemaphoreType.DMA
+    query_grad, key_grad, value_grad, weight_grad = pl.pallas_call(
+        functools.partial(kernel, depth, out_scale),
+        out_shape=(
+            jax.ShapeDtypeStruct(query_heads.shape[1:], BF16),
+            jax.ShapeDtypeStruct((rows, key_width), BF16),
+            jax.ShapeDtypeStruct((rows, key_width), BF16),
+            jax.ShapeDtypeStruct((width, key_width), F32),
+        ),
+        in_specs=[pl.BlockSpec(memory_space=pl.ANY)] * 5 + [pl.BlockSpec(memory_space=pltpu.SMEM)],
+        out_specs=(vmem,) * 4,
+        scratch_shapes=[
+            pltpu.VMEM(query_heads.shape[1:], BF16),
+            pltpu.VMEM((rows, key_width), BF16),
+            pltpu.VMEM((rows, key_width), BF16),
+            pltpu.VMEM(query_heads.shape[1:], BF16),
+            pltpu.VMEM((rows, key_width), BF16),
+            pltpu.VMEM((rows, key_width), BF16),
+            pltpu.VMEM((2 * rows, rows), F32),
+            pltpu.VMEM((KVH, rows, HD), BF16),
+            pltpu.VMEM((KVH, rows, HD), BF16),
+            pltpu.VMEM((depth, PLANE * rows, width), BF16),
+            pltpu.VMEM((key_width, PLANE * rows), BF16),
+            pltpu.VMEM((depth, key_width, width), BF16),
+            pltpu.VMEM((depth, key_width, width), BF16),
+            pltpu.VMEM((key_width, width), F32),
+            dma((4,)), dma((2, KVH)), dma((2, KVH)), dma((2, KVH)), dma((2, KVH)),
+            dma((depth, PLANE - 1)), dma((depth, PLANE - 1)), dma((depth,)),
+            dma((KVH, PLANE - 1)), dma((KVH, PLANE - 1)),
+            dma((depth, KVH)), dma((depth, KVH)),
+        ],
+        compiler_params=pltpu.CompilerParams(
+            collective_id=0, has_side_effects=True, vmem_limit_bytes=48 * 1024 * 1024
+        ),
+    )(query_heads[0], key_heads[0], value_heads[0], out_grad[0], layer_inputs[0], doc_lengths)
+    return (query_grad[None], key_grad[None], value_grad[None], weight_grad)
 
 
 def document_ids(lengths_row, length):
@@ -96,6 +435,16 @@
     return (query_grad[None], key_grad[None], value_grad[None], weight_grad)
 
 
+def place(query_heads, key_heads, value_heads, out_grad, layer_inputs, doc_lengths):
+    arrays = (query_heads, key_heads, value_heads, out_grad, layer_inputs, doc_lengths)
+    rows, model = layer_inputs.shape[1:]
+    count = lax.axis_size("dp") * lax.axis_size("ctx")
+    whole_tiles = rows % HD == 0 and model % (count * HD) == 0
+    if lax.axis_size("ctx") == 2 and count == PLANE * KVH and whole_tiles:
+        return fused(*arrays)
+    return shards(*arrays)
+
+
 def solution(mesh):
     placed = (
         P("dp", "ctx", None),
@@ -106,7 +455,7 @@
         P("dp", None),
     )
     return jax.shard_map(
-        shards,
+        place,
         mesh=mesh,
         in_specs=placed,
         out_specs=(

time: 439 us -> 78 us (0.18)
  the two profiles are of different devices: /device:TPU:11 before, /device:TPU:0 now
where the time goes in v2:
time: 78 us; the launch traced here: 77.8 us
  Pallas kernels  69.2 us (89%)
  local copies, waits for them, and re-layouts  7.98 us (10%)
    pallas_call x1, Pallas kernels, fused(): pl.pallas_call(functools.partial(kernel, depth, out_scale), out_shape=(ja...  69.2 us
    unnamed x14, local copies, waits for them, and re-layouts  7.98 us

profile of v2, /device:TPU:0, one launch (start us, length us, event | category | flops | bytes accessed | tf_op | source)
XLA Modules:
  0.0 77.8 jit_solution(16602690300256789608)
XLA Ops:
  0.6 0.0 copy-start
  0.6 1.2 %copy-done = bf16[1,128,4096]{2,1,0:T(8,128)(2,1)S(1)} copy-done((bf16[1,128,4096]{2,1,0:T(8,128)(2,1)S(1)}, bf16[1,128,4096]{2,1,0:T(8,128)(2,1)}, u32[]{:S(2)}) %copy-start) | copy-done | bytes 1048600
  1.9 0.0 copy-start.1
  1.9 1.2 %copy-done.1 = bf16[1,128,4096]{2,1,0:T(8,128)(2,1)S(1)} copy-done((bf16[1,128,4096]{2,1,0:T(8,128)(2,1)S(1)}, bf16[1,128,4096]{2,1,0:T(8,128)(2,1)}, u32[]{:S(2)}) %copy-start.1) | copy-done | bytes 1048600
  3.1 0.0 copy-start.2
  3.1 0.9 %copy-done.2 = bf16[1,128,512]{2,1,0:T(8,128)(2,1)S(1)} copy-done((bf16[1,128,512]{2,1,0:T(8,128)(2,1)S(1)}, bf16[1,128,512]{2,1,0:T(8,128)(2,1)}, u32[]{:S(2)}) %copy-start.2) | copy-done | bytes 131096
  4.0 0.0 copy-start.3
  4.0 0.9 %copy-done.3 = bf16[1,128,512]{2,1,0:T(8,128)(2,1)S(1)} copy-done((bf16[1,128,512]{2,1,0:T(8,128)(2,1)S(1)}, bf16[1,128,512]{2,1,0:T(8,128)(2,1)}, u32[]{:S(2)}) %copy-start.3) | copy-done | bytes 131096
  4.9 0.0 copy-start.4
  4.9 0.7 copy-done.4
  5.5 69.2 %shard_map.93 = (bf16[128,4096]{1,0:T(8,128)(2,1)S(1)}, bf16[128,512]{1,0:T(8,128)(2,1)S(1)}, bf16[128,512]{1,0:T(8,128)(2,1)S(1)}, f32[256,512]{1,0:T(8,128)S(1)}) custom-call(bf16[128,4096]{1,0:T(8,128)(2,1)S(1)} %bitcast.8, bf16[128,512]{1,0:T(8,128)(2,1)S(1)} %bitcast.11, bf16[128,512]{1,0:T(8,128)(2,1)S(1)} %bitcast.12, bf16[128,4096]{1,0:T(8,128)(2,1)S(1)} %bitcast.9, ...), custom_call_target="tpu_custom_call" | custom-call | tf_op jit(solution)/shard_map/pallas_call | solution.py:316
  74.7 1.0 %copy.14 = bf16[1,128,4096]{2,1,0:T(8,128)(2,1)} copy(bf16[1,128,4096]{2,1,0:T(8,128)(2,1)S(1)} %bitcast.10) | data formatting | bytes 2097152
  75.7 0.7 copy.15
  76.3 0.7 copy.16
  77.0 0.8 %copy.17 = f32[256,512]{1,0:T(8,128)} copy(f32[256,512]{1,0:T(8,128)S(1)} %get-tuple-element.19) | data formatting | bytes 1048576
Async XLA Ops:
  0.6 1.2 %copy-start = (bf16[1,128,4096]{2,1,0:T(8,128)(2,1)S(1)}, bf16[1,128,4096]{2,1,0:T(8,128)(2,1)}, u32[]{:S(2)}) copy-start(bf16[1,128,4096]{2,1,0:T(8,128)(2,1)} %param.6) | copy-start | bytes 3145732
  1.9 1.2 %copy-start.1 = (bf16[1,128,4096]{2,1,0:T(8,128)(2,1)S(1)}, bf16[1,128,4096]{2,1,0:T(8,128)(2,1)}, u32[]{:S(2)}) copy-start(bf16[1,128,4096]{2,1,0:T(8,128)(2,1)} %param.9) | copy-start | bytes 3145732
  3.1 0.9 %copy-start.2 = (bf16[1,128,512]{2,1,0:T(8,128)(2,1)S(1)}, bf16[1,128,512]{2,1,0:T(8,128)(2,1)}, u32[]{:S(2)}) copy-start(bf16[1,128,512]{2,1,0:T(8,128)(2,1)} %param.7) | copy-start | bytes 393220
  4.0 0.9 %copy-start.3 = (bf16[1,128,512]{2,1,0:T(8,128)(2,1)S(1)}, bf16[1,128,512]{2,1,0:T(8,128)(2,1)}, u32[]{:S(2)}) copy-start(bf16[1,128,512]{2,1,0:T(8,128)(2,1)} %param.8) | copy-start | bytes 393220
  4.9 0.7 copy-start.4

commit v3 on v2

--- a/solution.py
+++ b/solution.py
@@ -59,7 +59,7 @@
     q_hbm, k_hbm, v_hbm, go_hbm, x_ref, len_ref,
     dq_ref, dk_ref, dv_ref, w_ref,
     q_ref, k_ref, v_ref, go_ref, k_prev, v_prev, bias, term_k, term_v,
-    x_all, dvt_all, w_send, w_recv, w_own,
+    x_pack, x_all, dvt_all, w_send, w_recv, w_own,
     in_sem, kv_send, kv_recv, term_send, term_recv,
     x_send, x_recv, x_local, dv_send, dv_recv, ws_send, ws_recv,
 ):
@@ -73,71 +73,6 @@
     width = w_ref.shape[0]
     scale = HD ** -0.5
 
-    inputs = [
-        pltpu.make_async_copy(src, dst, in_sem.at[i])
-        for i, (src, dst) in enumerate(
-            [(k_hbm, k_ref), (v_hbm, v_ref), (q_hbm, q_ref), (go_hbm, go_ref)]
-        )
-    ]
-    for copy in inputs:
-        copy.start()
-
-    def peer(offset):
-        other = (me + offset) % PLANE
-        return other, (z * lanes + other // 2, other % 2)
-
-    def level(target):
-        return (target * lanes + lane, ctx)
-
-    partner = (dp, 1 - ctx)
-
-    barrier = pltpu.get_barrier_semaphore()
-    for offset in range(1, PLANE):
-        pl.semaphore_signal(barrier, inc=1, device_id=peer(offset)[1], device_id_type=MESH)
-    for step in range(1, depth):
-        pl.semaphore_signal(barrier, inc=1, device_id=level((z + step) % depth), device_id_type=MESH)
-    pl.semaphore_wait(barrier, PLANE - 1 + depth - 1)
-
-    def remote(src, dst, send, recv, device):
-        return pltpu.make_async_remote_copy(
-            src_ref=src, dst_ref=dst, send_sem=send, recv_sem=recv,
-            device_id=device, device_id_type=MESH,
-        )
-
-    def kv_copy(g, part):
-        src, dst = ((k_hbm, k_prev), (v_hbm, v_prev))[part]
-        here = cols(g)
-        return remote(src.at[:, here], dst.at[:, here], kv_send.at[part, g], kv_recv.at[part, g], partner)
-
-    def term_copy(g, part):
-        buffer = (term_v, term_k)[part].at[g]
-        return remote(buffer, buffer, term_send.at[part, g], term_recv.at[part, g], partner)
-
-    def x_copy(target, offset, sender, receiver, device):
-        return remote(
-            x_ref.at[:, cols(target * PLANE + receiver, width)],
-            x_all.at[target, pl.ds(pl.multiple_of(sender * rows, rows), rows)],
-            x_send.at[target, offset - 1], x_recv.at[target, offset - 1], device,
-        )
-
-    def own_copy(target):
-        return pltpu.make_async_copy(
-            x_ref.at[:, cols(target * PLANE + me, width)],
-            x_all.at[target, pl.ds(pl.multiple_of(me * rows, rows), rows)],
-            x_local.at[target],
-        )
-
-    def dv_copy(g, offset, sender, device):
-        place = dvt_all.at[cols(g), cols(sender, rows)]
-        return remote(place, place, dv_send.at[g, offset - 1], dv_recv.at[g, offset - 1], device)
-
-    def w_copy(g, source, target):
-        here = cols(g)
-        return remote(
-            w_send.at[target, here], w_recv.at[source, here],
-            ws_send.at[target, g], ws_recv.at[source, g], level(target),
-        )
-
     table = target_orders(depth)
 
     def target_at(step):
@@ -148,18 +83,87 @@
                 target = target + here * table[place][number]
         return target
 
+    targets = [target_at(step) for step in range(depth)]
+
+    def pack_copy(target, offset):
+        own = x_all.at[target, pl.ds(pl.multiple_of(me * rows, rows), rows)]
+        return pltpu.make_async_copy(
+            x_ref.at[:, cols(target * PLANE + (me + offset) % PLANE, width)],
+            x_pack.at[target, offset] if offset else own,
+            x_local.at[target, offset],
+        )
+
+    inputs = [
+        pltpu.make_async_copy(src, dst, in_sem.at[i])
+        for i, (src, dst) in enumerate(
+            [(k_hbm, k_ref), (v_hbm, v_ref), (q_hbm, q_ref), (go_hbm, go_ref)]
+        )
+    ]
+    for target in targets:
+        for offset in [*range(2, PLANE, 2), *range(1, PLANE, 2), 0]:
+            pack_copy(target, offset).start()
+    for copy in inputs:
+        copy.start()
+
+    def peer(offset):
+        other = (me + offset) % PLANE
+        return other, (z * lanes + other // 2, other % 2)
+
+    def level(target):
+        return (target * lanes + lane, ctx)
+
+    partner = (dp, 1 - ctx)
+
+    barrier = pltpu.get_barrier_semaphore()
+    for offset in range(1, PLANE):
+        pl.semaphore_signal(barrier, inc=1, device_id=peer(offset)[1], device_id_type=MESH)
+    for step in range(1, depth):
+        pl.semaphore_signal(barrier, inc=1, device_id=level((z + step) % depth), device_id_type=MESH)
+    pl.semaphore_wait(barrier, PLANE - 1 + depth - 1)
+
+    def remote(src, dst, send, recv, device):
+        return pltpu.make_async_remote_copy(
+            src_ref=src, dst_ref=dst, send_sem=send, recv_sem=recv,
+            device_id=device, device_id_type=MESH,
+        )
+
+    def kv_copy(g, part):
+        src, dst = ((k_hbm, k_prev), (v_hbm, v_prev))[part]
+        here = cols(g)
+        return remote(src.at[:, here], dst.at[:, here], kv_send.at[part, g], kv_recv.at[part, g], partner)
+
+    def term_copy(g, part):
+        buffer = (term_v, term_k)[part].at[g]
+        return remote(buffer, buffer, term_send.at[part, g], term_recv.at[part, g], partner)
+
+    def x_copy(target, offset, sender, device):
+        return remote(
+            x_pack.at[target, offset],
+            x_all.at[target, pl.ds(pl.multiple_of(sender * rows, rows), rows)],
+            x_send.at[target, offset - 1], x_recv.at[target, offset - 1], device,
+        )
+
+    def dv_copy(g, offset, sender, device):
+        place = dvt_all.at[g, sender]
+        return remote(place, place, dv_send.at[g, offset - 1], dv_recv.at[g, offset - 1], device)
+
+    def w_copy(g, source, target):
+        here = cols(g)
+        return remote(
+            w_send.at[target, here], w_recv.at[source, here],
+            ws_send.at[target, g], ws_recv.at[source, g], level(target),
+        )
+
     @pl.when(ctx == 0)
     def _():
         for g in range(KVH):
             for part in range(2):
                 kv_copy(g, part).start()
 
-    targets = [target_at(step) for step in range(depth)]
     for target in targets:
         for offset in range(2, PLANE, 2):
-            other, device = peer(offset)
-            x_copy(target, offset, me, other, device).start()
-        own_copy(target).start()
+            pack_copy(target, offset).wait()
+            x_copy(target, offset, me, peer(offset)[1]).start()
 
     @pl.when(ctx == 0)
     def _():
@@ -169,8 +173,8 @@
 
     for target in targets:
         for offset in range(1, PLANE, 2):
-            other, device = peer(offset)
-            x_copy(target, offset, me, other, device).start()
+            pack_copy(target, offset).wait()
+            x_copy(target, offset, me, peer(offset)[1]).start()
 
     for copy in inputs:
         copy.wait()
@@ -216,7 +220,10 @@
         here = cols(g)
         dk_ref[:, here] = key_sum.astype(BF16)
         dv_ref[:, here] = value_sum.astype(BF16)
-        dvt_all[here, cols(me, rows)] = value_sum.T.astype(BF16)
+        dvt_all[g, me] = value_sum.T.astype(BF16)
+
+    def gathered(g):
+        return jnp.concatenate([dvt_all[g, sender] for sender in range(PLANE)], axis=1)
 
     def shell(m):
         for offset in range(1, PLANE):
@@ -233,7 +240,7 @@
             def _():
                 x_wait(target)
 
-            product = nn(dvt_all[cols(g)], x_all[target])
+            product = nn(gathered(g), x_all[target])
             w_send[target, cols(g)] = product.astype(BF16)
             w_copy(g, z, target).start()
             return carry
@@ -244,8 +251,8 @@
     def x_wait(target):
         for offset in range(1, PLANE):
             sender = (me + PLANE - offset) % PLANE
-            x_copy(target, offset, sender, me, peer(offset)[1]).wait_recv()
-        own_copy(target).wait()
+            x_copy(target, offset, sender, peer(offset)[1]).wait_recv()
+        pack_copy(target, 0).wait()
 
     def group(g, carry):
         @pl.when(ctx == 0)
@@ -278,7 +285,7 @@
     lax.fori_loop(0, KVH, group, 0)
     shell(jnp.int32(KVH - 1))
     x_wait(z)
-    w_own[...] = nn(dvt_all[...], x_all[z])
+    w_own[...] = nn(jnp.concatenate([gathered(g) for g in range(KVH)], axis=0), x_all[z])
     for step in range(1, depth):
         source = (z + step) % depth
         for g in range(KVH):
@@ -288,8 +295,7 @@
 
     for target in targets:
         for offset in range(1, PLANE):
-            other, device = peer(offset)
-            x_copy(target, offset, me, other, device).wait_send()
+            x_copy(target, offset, me, peer(offset)[1]).wait_send()
     for step in range(1, depth):
         for g in range(KVH):
             w_copy(g, z, (z + step) % depth).wait_send()
@@ -321,7 +327,7 @@
             jax.ShapeDtypeStruct((rows, key_width), BF16),
             jax.ShapeDtypeStruct((width, key_width), F32),
         ),
-        in_specs=[pl.BlockSpec(memory_space=pl.ANY)] * 5 + [pl.BlockSpec(memory_space=pltpu.SMEM)],
+        in_specs=[pl.BlockSpec(memory_space=pltpu.HBM)] * 5 + [pl.BlockSpec(memory_space=pltpu.SMEM)],
         out_specs=(vmem,) * 4,
         scratch_shapes=[
             pltpu.VMEM(query_heads.shape[1:], BF16),
@@ -333,18 +339,19 @@
             pltpu.VMEM((2 * rows, rows), F32),
             pltpu.VMEM((KVH, rows, HD), BF16),
             pltpu.VMEM((KVH, rows, HD), BF16),
+            pltpu.VMEM((depth, PLANE, rows, width), BF16),
             pltpu.VMEM((depth, PLANE * rows, width), BF16),
-            pltpu.VMEM((key_width, PLANE * rows), BF16),
+            pltpu.VMEM((KVH, PLANE, HD, rows), BF16),
             pltpu.VMEM((depth, key_width, width), BF16),
             pltpu.VMEM((depth, key_width, width), BF16),
             pltpu.VMEM((key_width, width), F32),
             dma((4,)), dma((2, KVH)), dma((2, KVH)), dma((2, KVH)), dma((2, KVH)),
-            dma((depth, PLANE - 1)), dma((depth, PLANE - 1)), dma((depth,)),
+            dma((depth, PLANE - 1)), dma((depth, PLANE - 1)), dma((depth, PLANE)),
             dma((KVH, PLANE - 1)), dma((KVH, PLANE - 1)),
             dma((depth, KVH)), dma((depth, KVH)),
         ],
         compiler_params=pltpu.CompilerParams(
-            collective_id=0, has_side_effects=True, vmem_limit_bytes=48 * 1024 * 1024
+            collective_id=0, has_side_effects=True, vmem_limit_bytes=64 * 1024 * 1024
         ),
     )(query_heads[0], key_heads[0], value_heads[0], out_grad[0], layer_inputs[0], doc_lengths)
     return (query_grad[None], key_grad[None], value_grad[None], weight_grad)

time: 78 us -> 75.9 us (0.973)
  local copies, waits for them, and re-layouts: 7.98 us -> 4.47 us
  Pallas kernels: 69.2 us -> 70.7 us
    unnamed x14 -> x10, local copies, waits for them, and re-layouts: 7.98 us -> 4.47 us
    pallas_call x1, Pallas kernels: 69.2 us -> 70.7 us  [fused(): pl.pallas_call(functools.partial(kernel, depth, out_scale), out_shape=(ja...]
where the time goes in v3:
time: 75.9 us; the launch traced here: 75.8 us
  Pallas kernels  70.7 us (93%)
  local copies, waits for them, and re-layouts  4.47 us (6%)
    pallas_call x1, Pallas kernels, fused(): pl.pallas_call(functools.partial(kernel, depth, out_scale), out_shape=(ja...  70.7 us
    unnamed x10, local copies, waits for them, and re-layouts  4.47 us

profile of v3, /device:TPU:0, one launch (start us, length us, event | category | flops | bytes accessed | tf_op | source)
XLA Modules:
  0.0 75.8 jit_solution(11344062081661847035)
XLA Ops:
  0.6 70.7 %shard_map.93 = (bf16[128,4096]{1,0:T(8,128)(2,1)}, bf16[128,512]{1,0:T(8,128)(2,1)}, bf16[128,512]{1,0:T(8,128)(2,1)}, f32[256,512]{1,0:T(8,128)}) custom-call(bf16[128,4096]{1,0:T(8,128)(2,1)} %bitcast.9, bf16[128,512]{1,0:T(8,128)(2,1)} %bitcast.12, bf16[128,512]{1,0:T(8,128)(2,1)} %bitcast.13, bf16[128,4096]{1,0:T(8,128)(2,1)} %bitcast.10, ...), custom_call_target="tpu_custom_call" | custom-call | tf_op jit(solution)/shard_map/pallas_call | solution.py:322
  71.3 0.0 copy-start.2
  71.3 0.0 copy-start.1
  71.3 0.0 copy-start
  71.3 2.4 %copy.14 = bf16[1,128,4096]{2,1,0:T(8,128)(2,1)} copy(bf16[1,128,4096]{2,1,0:T(8,128)(2,1)} %bitcast.11) | data formatting | bytes 2097152
  73.7 0.0 copy-done.2
  73.7 0.7 copy.15
  74.3 0.0 copy-done.1
  74.3 0.7 copy.16
  75.0 0.0 copy-done
  75.0 0.8 %copy.17 = f32[256,512]{1,0:T(8,128)} copy(f32[256,512]{1,0:T(8,128)S(1)} %copy-done) | data formatting | bytes 1048576
Async XLA Ops:
  71.3 2.4 %copy-start.2 = (bf16[128,512]{1,0:T(8,128)(2,1)S(1)}, bf16[128,512]{1,0:T(8,128)(2,1)}, u32[]{:S(2)}) copy-start(bf16[128,512]{1,0:T(8,128)(2,1)} %get-tuple-element.9) | copy-start | bytes 393220
  71.3 3.0 %copy-start.1 = (bf16[128,512]{1,0:T(8,128)(2,1)S(1)}, bf16[128,512]{1,0:T(8,128)(2,1)}, u32[]{:S(2)}) copy-start(bf16[128,512]{1,0:T(8,128)(2,1)} %get-tuple-element.10) | copy-start | bytes 393220
  71.3 3.7 %copy-start = (f32[256,512]{1,0:T(8,128)S(1)}, f32[256,512]{1,0:T(8,128)}, u32[]{:S(2)}) copy-start(f32[256,512]{1,0:T(8,128)} %get-tuple-element.19) | copy-start | bytes 1572868

commit v4 on v3

--- a/solution.py
+++ b/solution.py
@@ -160,10 +160,16 @@
             for part in range(2):
                 kv_copy(g, part).start()
 
-    for target in targets:
-        for offset in range(2, PLANE, 2):
-            pack_copy(target, offset).wait()
-            x_copy(target, offset, me, peer(offset)[1]).start()
+    def x_start(step, offset):
+        x_copy(target_at(step), offset, me, peer(offset)[1]).start()
+
+    def x_packed(step):
+        for offset in range(1, PLANE):
+            pack_copy(targets[step], offset).wait()
+
+    x_packed(0)
+    for offset in range(2, PLANE, 2):
+        x_start(0, offset)
 
     @pl.when(ctx == 0)
     def _():
@@ -171,10 +177,10 @@
             for part in range(2):
                 kv_copy(g, part).wait_send()
 
-    for target in targets:
-        for offset in range(1, PLANE, 2):
-            pack_copy(target, offset).wait()
-            x_copy(target, offset, me, peer(offset)[1]).start()
+    for offset in range(1, PLANE, 2):
+        x_start(0, offset)
+    for step in range(1, depth):
+        x_packed(step)
 
     for copy in inputs:
         copy.wait()
@@ -225,28 +231,16 @@
     def gathered(g):
         return jnp.concatenate([dvt_all[g, sender] for sender in range(PLANE)], axis=1)
 
-    def shell(m):
+    def gather_wait(g):
         for offset in range(1, PLANE):
             sender = (me + PLANE - offset) % PLANE
-            dv_copy(m, offset, sender, peer(offset)[1]).wait_recv()
-
-        def block(i, carry):
-            old = (i < m).astype(jnp.int32)
-            step = old * i + (1 - old) * m
-            g = old * m + (1 - old) * (i - m)
-            target = target_at(step)
-
-            @pl.when(i == m)
-            def _():
-                x_wait(target)
-
-            product = nn(gathered(g), x_all[target])
-            w_send[target, cols(g)] = product.astype(BF16)
-            w_copy(g, z, target).start()
-            return carry
-
-        last = (m == depth - 1).astype(jnp.int32)
-        lax.fori_loop(0, 2 * m + 1 - last * (m + 1), block, 0)
+            dv_copy(g, offset, sender, peer(offset)[1]).wait_recv()
+
+    def first_block(g):
+        gather_wait(g)
+        target = targets[0]
+        w_send[target, cols(g)] = nn(gathered(g), x_all[target]).astype(BF16)
+        w_copy(g, z, target).start()
 
     def x_wait(target):
         for offset in range(1, PLANE):
@@ -255,6 +249,12 @@
         pack_copy(target, 0).wait()
 
     def group(g, carry):
+        x_start(1, 2 * g + 1)
+
+        @pl.when(2 * g + 2 < PLANE)
+        def _():
+            x_start(1, 2 * g + 2)
+
         @pl.when(ctx == 0)
         def _():
             key_sum, value_sum = attend(g, 1)
@@ -276,14 +276,32 @@
         for offset in range(1, PLANE):
             dv_copy(g, offset, me, peer(offset)[1]).start()
 
+        @pl.when(g == 1)
+        def _():
+            x_wait(targets[0])
+
         @pl.when(g > 0)
         def _():
-            shell(g - 1)
+            first_block(g - 1)
 
         return carry
 
     lax.fori_loop(0, KVH, group, 0)
-    shell(jnp.int32(KVH - 1))
+    for step in range(2, depth):
+        for offset in range(1, PLANE):
+            x_start(step, offset)
+    first_block(KVH - 1)
+
+    def later(step, carry):
+        target = target_at(step)
+        x_wait(target)
+        spread = jnp.concatenate([gathered(g) for g in range(KVH)], axis=0)
+        w_send[target] = nn(spread, x_all[target]).astype(BF16)
+        for g in range(KVH):
+            w_copy(g, z, target).start()
+        return carry
+
+    lax.fori_loop(1, depth - 1, later, 0)
     x_wait(z)
     w_own[...] = nn(jnp.concatenate([gathered(g) for g in range(KVH)], axis=0), x_all[z])
     for step in range(1, depth):

time: 75.9 us -> 64.8 us (0.85)
  the two profiles are of different devices: /device:TPU:0 before, /device:TPU:11 now
where the time goes in v4:
time: 64.8 us; the launch traced here: 64.6 us
  Pallas kernels  59.5 us (92%)
  local copies, waits for them, and re-layouts  4.47 us (7%)
  between operations  0.67 us (1%)
    pallas_call x1, Pallas kernels, fused(): pl.pallas_call(functools.partial(kernel, depth, out_scale), out_shape=(ja...  59.5 us
    unnamed x10, local copies, waits for them, and re-layouts  4.47 us

profile of v4, /device:TPU:11, one launch (start us, length us, event | category | flops | bytes accessed | tf_op | source)
XLA Modules:
  0.0 64.6 jit_solution(3439109541550572663)
XLA Ops:
  0.6 59.5 %shard_map.93 = (bf16[128,4096]{1,0:T(8,128)(2,1)}, bf16[128,512]{1,0:T(8,128)(2,1)}, bf16[128,512]{1,0:T(8,128)(2,1)}, f32[256,512]{1,0:T(8,128)}) custom-call(bf16[128,4096]{1,0:T(8,128)(2,1)} %bitcast.9, bf16[128,512]{1,0:T(8,128)(2,1)} %bitcast.12, bf16[128,512]{1,0:T(8,128)(2,1)} %bitcast.13, bf16[128,4096]{1,0:T(8,128)(2,1)} %bitcast.10, ...), custom_call_target="tpu_custom_call" | custom-call | tf_op jit(solution)/shard_map/pallas_call | solution.py:340
  60.1 0.0 copy-start.2
  60.1 0.0 copy-start.1
  60.2 0.0 copy-start
  60.2 2.4 %copy.14 = bf16[1,128,4096]{2,1,0:T(8,128)(2,1)} copy(bf16[1,128,4096]{2,1,0:T(8,128)(2,1)} %bitcast.11) | data formatting | bytes 2097152
  62.5 0.0 copy-done.2
  62.5 0.7 %copy.15 = bf16[1,128,512]{2,1,0:T(8,128)(2,1)} copy(bf16[1,128,512]{2,1,0:T(8,128)(2,1)S(1)} %bitcast.15) | data formatting | bytes 262144
  63.2 0.0 copy-done.1
  63.2 0.7 %copy.16 = bf16[1,128,512]{2,1,0:T(8,128)(2,1)} copy(bf16[1,128,512]{2,1,0:T(8,128)(2,1)S(1)} %bitcast.14) | data formatting | bytes 262144
  63.8 0.0 copy-done
  63.8 0.8 %copy.17 = f32[256,512]{1,0:T(8,128)} copy(f32[256,512]{1,0:T(8,128)S(1)} %copy-done) | data formatting | bytes 1048576
Async XLA Ops:
  60.1 2.4 %copy-start.2 = (bf16[128,512]{1,0:T(8,128)(2,1)S(1)}, bf16[128,512]{1,0:T(8,128)(2,1)}, u32[]{:S(2)}) copy-start(bf16[128,512]{1,0:T(8,128)(2,1)} %get-tuple-element.9) | copy-start | bytes 393220
  60.1 3.0 %copy-start.1 = (bf16[128,512]{1,0:T(8,128)(2,1)S(1)}, bf16[128,512]{1,0:T(8,128)(2,1)}, u32[]{:S(2)}) copy-start(bf16[128,512]{1,0:T(8,128)(2,1)} %get-tuple-element.10) | copy-start | bytes 393220
  60.2 3.7 %copy-start = (f32[256,512]{1,0:T(8,128)S(1)}, f32[256,512]{1,0:T(8,128)}, u32[]{:S(2)}) copy-start(f32[256,512]{1,0:T(8,128)} %get-tuple-element.19) | copy-start | bytes 1572868

commit v5 on v4

--- a/solution.py
+++ b/solution.py
@@ -143,9 +143,30 @@
             x_send.at[target, offset - 1], x_recv.at[target, offset - 1], device,
         )
 
-    def dv_copy(g, offset, sender, device):
-        place = dvt_all.at[g, sender]
-        return remote(place, place, dv_send.at[g, offset - 1], dv_recv.at[g, offset - 1], device)
+    def flip(bits):
+        row, core = (lane // 2 + bits // 4) % 2, (lane % 2 + bits // 2 % 2) % 2
+        other = row * 4 + core * 2 + (ctx + bits % 2) % 2
+        return other, (z * lanes + other // 2, other % 2)
+
+    def dv_copy(g, bits, block, device):
+        place = dvt_all.at[g, block]
+        return remote(place, place, dv_send.at[g, bits - 1], dv_recv.at[g, bits - 1], device)
+
+    def dv_direct(g):
+        return [dv_copy(g, bits, me, flip(bits)[1]) for bits in (1, 4, 5, 2)]
+
+    def dv_forward(g):
+        return [dv_copy(g, bits + 2, flip(bits)[0], flip(2)[1]) for bits in (1, 4, 5)]
+
+    def dv_arrived(g, kinds):
+        for bits in kinds:
+            other, device = flip(bits)
+            dv_copy(g, bits, other, device).wait_recv()
+
+    def forward(g):
+        dv_arrived(g, (1, 4, 5))
+        for copy in dv_forward(g):
+            copy.start()
 
     def w_copy(g, source, target):
         here = cols(g)
@@ -231,13 +252,8 @@
     def gathered(g):
         return jnp.concatenate([dvt_all[g, sender] for sender in range(PLANE)], axis=1)
 
-    def gather_wait(g):
-        for offset in range(1, PLANE):
-            sender = (me + PLANE - offset) % PLANE
-            dv_copy(g, offset, sender, peer(offset)[1]).wait_recv()
-
     def first_block(g):
-        gather_wait(g)
+        dv_arrived(g, (2, 3, 6, 7))
         target = targets[0]
         w_send[target, cols(g)] = nn(gathered(g), x_all[target]).astype(BF16)
         w_copy(g, z, target).start()
@@ -273,23 +289,29 @@
                 term_copy(g, part).start()
             finish(g, key_sum[rows:], value_sum[rows:])
 
-        for offset in range(1, PLANE):
-            dv_copy(g, offset, me, peer(offset)[1]).start()
-
-        @pl.when(g == 1)
+        for copy in dv_direct(g):
+            copy.start()
+
+        @pl.when(g > 0)
+        def _():
+            forward(g - 1)
+
+        @pl.when(g == 2)
         def _():
             x_wait(targets[0])
 
-        @pl.when(g > 0)
+        @pl.when(g > 1)
         def _():
-            first_block(g - 1)
+            first_block(g - 2)
 
         return carry
 
     lax.fori_loop(0, KVH, group, 0)
+    forward(KVH - 1)
     for step in range(2, depth):
         for offset in range(1, PLANE):
             x_start(step, offset)
+    first_block(KVH - 2)
     first_block(KVH - 1)
 
     def later(step, carry):
@@ -318,8 +340,8 @@
         for g in range(KVH):
             w_copy(g, z, (z + step) % depth).wait_send()
     for g in range(KVH):
-        for offset in range(1, PLANE):
-            dv_copy(g, offset, me, peer(offset)[1]).wait_send()
+        for copy in dv_direct(g) + dv_forward(g):
+            copy.wait_send()
 
     @pl.when(ctx == 1)
     def _():

time: 64.8 us -> 61.8 us (0.954)
  Pallas kernels: 59.5 us -> 56.5 us
    pallas_call x1, Pallas kernels: 59.5 us -> 56.5 us  [fused(): pl.pallas_call(functools.partial(kernel, depth, out_scale), out_shape=(ja...]
where the time goes in v5:
time: 61.8 us; the launch traced here: 61.6 us
  Pallas kernels  56.5 us (91%)
  local copies, waits for them, and re-layouts  4.47 us (7%)
  between operations  0.67 us (1%)
    pallas_call x1, Pallas kernels, fused(): pl.pallas_call(functools.partial(kernel, depth, out_scale), out_shape=(ja...  56.5 us
    unnamed x10, local copies, waits for them, and re-layouts  4.47 us

profile of v5, /device:TPU:11, one launch (start us, length us, event | category | flops | bytes accessed | tf_op | source)
XLA Modules:
  0.0 61.6 jit_solution(4820177017673181671)
XLA Ops:
  0.6 56.5 %shard_map.93 = (bf16[128,4096]{1,0:T(8,128)(2,1)}, bf16[128,512]{1,0:T(8,128)(2,1)}, bf16[128,512]{1,0:T(8,128)(2,1)}, f32[256,512]{1,0:T(8,128)}) custom-call(bf16[128,4096]{1,0:T(8,128)(2,1)} %bitcast.9, bf16[128,512]{1,0:T(8,128)(2,1)} %bitcast.12, bf16[128,512]{1,0:T(8,128)(2,1)} %bitcast.13, bf16[128,4096]{1,0:T(8,128)(2,1)} %bitcast.10, ...), custom_call_target="tpu_custom_call" | custom-call | tf_op jit(solution)/shard_map/pallas_call | solution.py:362
  57.1 0.0 copy-start.2
  57.1 0.0 copy-start.1
  57.2 0.0 copy-start
  57.2 2.4 %copy.14 = bf16[1,128,4096]{2,1,0:T(8,128)(2,1)} copy(bf16[1,128,4096]{2,1,0:T(8,128)(2,1)} %bitcast.11) | data formatting | bytes 2097152
  59.5 0.0 copy-done.2
  59.5 0.7 %copy.15 = bf16[1,128,512]{2,1,0:T(8,128)(2,1)} copy(bf16[1,128,512]{2,1,0:T(8,128)(2,1)S(1)} %bitcast.15) | data formatting | bytes 262144
  60.2 0.0 copy-done.1
  60.2 0.7 %copy.16 = bf16[1,128,512]{2,1,0:T(8,128)(2,1)} copy(bf16[1,128,512]{2,1,0:T(8,128)(2,1)S(1)} %bitcast.14) | data formatting | bytes 262144
  60.8 0.0 copy-done
  60.8 0.8 %copy.17 = f32[256,512]{1,0:T(8,128)} copy(f32[256,512]{1,0:T(8,128)S(1)} %copy-done) | data formatting | bytes 1048576
Async XLA Ops:
  57.1 2.4 %copy-start.2 = (bf16[128,512]{1,0:T(8,128)(2,1)S(1)}, bf16[128,512]{1,0:T(8,128)(2,1)}, u32[]{:S(2)}) copy-start(bf16[128,512]{1,0:T(8,128)(2,1)} %get-tuple-element.9) | copy-start | bytes 393220
  57.1 3.0 %copy-start.1 = (bf16[128,512]{1,0:T(8,128)(2,1)S(1)}, bf16[128,512]{1,0:T(8,128)(2,1)}, u32[]{:S(2)}) copy-start(bf16[128,512]{1,0:T(8,128)(2,1)} %get-tuple-element.10) | copy-start | bytes 393220
  57.2 3.7 %copy-start = (f32[256,512]{1,0:T(8,128)S(1)}, f32[256,512]{1,0:T(8,128)}, u32[]{:S(2)}) copy-start(f32[256,512]{1,0:T(8,128)} %get-tuple-element.19) | copy-start | bytes 1572868

commit v6 on v5

--- a/solution.py
+++ b/solution.py
@@ -14,6 +14,7 @@
 GROUP = HEADS // KVH
 PAIR = 2
 PLANE = 8
+PACE = 3
 LOG2E = math.log2(math.e)
 F32 = jnp.float32
 BF16 = jnp.bfloat16
@@ -265,11 +266,9 @@
         pack_copy(target, 0).wait()
 
     def group(g, carry):
-        x_start(1, 2 * g + 1)
-
-        @pl.when(2 * g + 2 < PLANE)
-        def _():
-            x_start(1, 2 * g + 2)
+        for part in range(PACE):
+            number = g * PACE + part
+            x_start(1 + number // (PLANE - 1), number % (PLANE - 1) + 1)
 
         @pl.when(ctx == 0)
         def _():
@@ -308,9 +307,8 @@
 
     lax.fori_loop(0, KVH, group, 0)
     forward(KVH - 1)
-    for step in range(2, depth):
-        for offset in range(1, PLANE):
-            x_start(step, offset)
+    for number in range(KVH * PACE, (depth - 1) * (PLANE - 1)):
+        x_start(1 + number // (PLANE - 1), number % (PLANE - 1) + 1)
     first_block(KVH - 2)
     first_block(KVH - 1)
 

time: 61.8 us -> 65.1 us (1.053)
  Pallas kernels: 56.5 us -> 59.8 us
    pallas_call x1, Pallas kernels: 56.5 us -> 59.8 us  [fused(): pl.pallas_call(functools.partial(kernel, depth, out_scale), out_shape=(ja...]
where the time goes in v6:
time: 65.1 us; the launch traced here: 64.9 us
  Pallas kernels  59.8 us (92%)
  local copies, waits for them, and re-layouts  4.47 us (7%)
  between operations  0.67 us (1%)
    pallas_call x1, Pallas kernels, fused(): pl.pallas_call(functools.partial(kernel, depth, out_scale), out_shape=(ja...  59.8 us
    unnamed x10, local copies, waits for them, and re-layouts  4.47 us

profile of v6, /device:TPU:11, one launch (start us, length us, event | category | flops | bytes accessed | tf_op | source)
XLA Modules:
  0.0 64.9 jit_solution(14862210890103568368)
XLA Ops:
  0.6 59.8 %shard_map.93 = (bf16[128,4096]{1,0:T(8,128)(2,1)}, bf16[128,512]{1,0:T(8,128)(2,1)}, bf16[128,512]{1,0:T(8,128)(2,1)}, f32[256,512]{1,0:T(8,128)}) custom-call(bf16[128,4096]{1,0:T(8,128)(2,1)} %bitcast.9, bf16[128,512]{1,0:T(8,128)(2,1)} %bitcast.12, bf16[128,512]{1,0:T(8,128)(2,1)} %bitcast.13, bf16[128,4096]{1,0:T(8,128)(2,1)} %bitcast.10, ...), custom_call_target="tpu_custom_call" | custom-call | tf_op jit(solution)/shard_map/pallas_call | solution.py:360
  60.4 0.0 copy-start.2
  60.4 0.0 copy-start.1
  60.4 0.0 copy-start
  60.4 2.4 %copy.14 = bf16[1,128,4096]{2,1,0:T(8,128)(2,1)} copy(bf16[1,128,4096]{2,1,0:T(8,128)(2,1)} %bitcast.11) | data formatting | bytes 2097152
  62.8 0.0 copy-done.2
  62.8 0.7 %copy.15 = bf16[1,128,512]{2,1,0:T(8,128)(2,1)} copy(bf16[1,128,512]{2,1,0:T(8,128)(2,1)S(1)} %bitcast.15) | data formatting | bytes 262144
  63.5 0.0 copy-done.1
  63.5 0.7 %copy.16 = bf16[1,128,512]{2,1,0:T(8,128)(2,1)} copy(bf16[1,128,512]{2,1,0:T(8,128)(2,1)S(1)} %bitcast.14) | data formatting | bytes 262144
  64.1 0.0 copy-done
  64.1 0.8 %copy.17 = f32[256,512]{1,0:T(8,128)} copy(f32[256,512]{1,0:T(8,128)S(1)} %copy-done) | data formatting | bytes 1048576
Async XLA Ops:
  60.4 2.4 %copy-start.2 = (bf16[128,512]{1,0:T(8,128)(2,1)S(1)}, bf16[128,512]{1,0:T(8,128)(2,1)}, u32[]{:S(2)}) copy-start(bf16[128,512]{1,0:T(8,128)(2,1)} %get-tuple-element.9) | copy-start | bytes 393220
  60.4 3.0 %copy-start.1 = (bf16[128,512]{1,0:T(8,128)(2,1)S(1)}, bf16[128,512]{1,0:T(8,128)(2,1)}, u32[]{:S(2)}) copy-start(bf16[128,512]{1,0:T(8,128)(2,1)} %get-tuple-element.10) | copy-start | bytes 393220
  60.4 3.7 %copy-start = (f32[256,512]{1,0:T(8,128)S(1)}, f32[256,512]{1,0:T(8,128)}, u32[]{:S(2)}) copy-start(f32[256,512]{1,0:T(8,128)} %get-tuple-element.19) | copy-start | bytes 1572868
